TPU v7x, 256 devices: a whole 4x4x8 slice. The times are simulated.
256 devices in a mesh: dp: 4 (over y_hi, core), ctx: 8 (over z), tp: 8 (over y_lo, x).
Axes of the slice: x: 4, y: 4 (y_hi: 2, y_lo: 2; y = y_hi * 2 + y_lo), z: 8, core: 2. Of those that a mesh axis runs over, the one named last changes fastest.
Arguments:
- q_lat: bfloat16 [4, 1536, 128, 512], P('dp', 'ctx', 'tp'), may hold values from -36 to 36
- q_rope: bfloat16 [4, 1536, 8192], P('dp', 'ctx', 'tp'), may hold values from -4 to 4
- latent: bfloat16 [4, 1536, 512], P('dp', ('ctx', 'tp')), may hold values from -4 to 4
- k_rope: bfloat16 [4, 1536, 64], P('dp', ('ctx', 'tp')), may hold values from -4 to 4
- d_out: bfloat16 [4, 1536, 16384], P('dp', 'ctx', 'tp'), may hold values from -0.078125 to 0.078125
- w_uv: bfloat16 [128, 512, 128], P('tp'), may hold values from -0.25 to 0.25
- doc_lengths: int32 [4, 8], P('dp'), may hold values from 1 to 384, 1536 in all within a row
- block_order: int32 [4, 24], P('dp'), may hold values from 0 to 23, as said below
Outputs:
- attn_out: bfloat16 [4, 1536, 16384], P('dp', 'ctx', 'tp')
- grad_uv: float32 [512, 128, 128], P(('dp', 'ctx'), 'tp')
Inputs may be any that keep to these rules, and one draw needn't show every extreme that they name: `block_order`: each row is a permutation of the block numbers 0 to 23; the index k of ctx holds the blocks listed at places k * 3 to (k+1) * 3 - 1.
All inputs are finite; a program needn't handle non-finite values.
Results may differ from a plain program's by a relative error of at most 0.0052.
Values may be sent and summed in bfloat16 or wider, within the bound.
A program may use at most 128 MiB of HBM per device.

v0:
```python
import jax
import jax.numpy as jnp
from jax import lax
from jax.sharding import PartitionSpec as P

ROPE = 64
NOPE = 128
BLOCK = 64


def document_index(positions, ends):
    return jnp.sum((positions[:, None] >= ends[None, :]).astype(jnp.int32), axis=1)


def attend(query_lat, query_rope, query_pos, key_lat, key_rope, key_pos, ends):
    count, heads = (query_lat.shape[0], query_lat.shape[1])
    rotary = key_rope.shape[1]
    scores = jnp.einsum("rhc,nc->hrn", query_lat, key_lat, preferred_element_type=jnp.float32)
    scores = scores + jnp.einsum(
        "rhc,nc->hrn",
        query_rope.reshape(count, heads, rotary),
        key_rope,
        preferred_element_type=jnp.float32,
    )
    scores = scores * (NOPE + ROPE) ** (-0.5)
    same_doc = document_index(query_pos, ends)[:, None] == document_index(key_pos, ends)[None, :]
    allowed = same_doc & (key_pos[None, :] <= query_pos[:, None])
    scores = jnp.where(allowed[None], scores, -jnp.inf)
    top = jnp.max(scores, axis=2, keepdims=True)
    probs = jnp.exp(scores - top)
    total = jnp.sum(probs, axis=2)
    mixed = jnp.einsum(
        "hrn,nc->rhc", probs.astype(jnp.bfloat16), key_lat, preferred_element_type=jnp.float32
    )
    return (mixed / jnp.transpose(total)[:, :, None]).astype(jnp.bfloat16)


def on_device(q_lat, q_rope, latent, k_rope, d_out, w_uv, doc_lengths, block_order):
    rows, heads, width = (q_lat.shape[1], q_lat.shape[2], q_lat.shape[3])
    value_dim = w_uv.shape[2]
    blocks_here = rows // BLOCK
    place = lax.axis_index("ctx")
    owned = lax.dynamic_slice_in_dim(block_order[0], place * blocks_here, blocks_here)
    offsets = jnp.arange(rows, dtype=jnp.int32)
    positions = jnp.repeat(owned, BLOCK) * BLOCK + offsets % BLOCK
    ends = jnp.cumsum(doc_lengths[0])
    keys_lat, keys_rope = (
        lax.all_gather(latent[0], ("ctx", "tp"), axis=0, tiled=True),
        lax.all_gather(k_rope[0], ("ctx", "tp"), axis=0, tiled=True),
    )
    window = keys_lat.shape[0]
    key_pos = jnp.arange(window, dtype=jnp.int32)
    mixed = attend(q_lat[0], q_rope[0], positions, keys_lat, keys_rope, key_pos, ends)
    attn = jnp.einsum("rhc,hcv->rhv", mixed, w_uv, preferred_element_type=jnp.float32).astype(
        jnp.bfloat16
    )
    attn = attn.reshape(1, rows, heads * value_dim)
    grads_out = d_out[0].reshape(rows, heads, value_dim)
    grad = lax.psum_scatter(
        jnp.einsum("rhc,rhv->chv", mixed, grads_out, preferred_element_type=jnp.float32),
        ("dp", "ctx"),
        scatter_dimension=0,
        tiled=True,
    )
    return (attn, grad)


def solution(mesh):
    return jax.shard_map(
        on_device,
        mesh=mesh,
        in_specs=(
            P("dp", "ctx", "tp", None),
            P("dp", "ctx", "tp"),
            P("dp", ("ctx", "tp"), None),
            P("dp", ("ctx", "tp"), None),
            P("dp", "ctx", "tp"),
            P("tp", None, None),
            P("dp", None),
            P("dp", None),
        ),
        out_specs=(P("dp", "ctx", "tp"), P(("dp", "ctx"), "tp", None)),
        check_vma=False,
    )
```

profile of v0, /device:TPU:1, one launch (start us, length us, event | category | flops | bytes accessed | tf_op | source)
XLA Modules:
  0.0 490.0 jit_solution(15421976996216495866)
XLA Ops:
  7.2 0.0 copy-start
  7.2 0.0 all-gather.4.cloned.1.call-start
  7.2 0.7 all-gather.4.cloned.1.call-update
  7.9 0.0 reduce-scatter.2.cloned.1.call-start
  8.0 0.9 multiply_bitcast_fusion
  8.8 0.1 broadcast_in_dim.10
  8.9 0.1 mul.35
  9.0 0.8 reduce-window.8
  9.8 2.0 copy.29
  11.8 2.2 copy.33
  14.0 136.1 %all-gather.1 = bf16[1,1536,64]{2,1,0:T(8,128)(2,1)S(1)} all-gather(bf16[1,24,64]{2,1,0:T(8,128)(2,1)} %param.11), channel_id=3, replica_groups=mesh['dp'=4,'ctx'=8,'tp'=8] {'ctx','tp'}, dimensions={1}, use_global_device_ids=true | all-gather | bytes 199680 | tf_op jit(solution)/shard_map/all_gather | solution.py:49
  150.1 0.1 convert_reduce_fusion
  150.2 0.1 convert_reduce_fusion.1
  150.3 1.2 fusion.13
  151.4 116.6 %all-gather.4.cloned.1.call-done = bf16[1,1536,512]{2,1,0:T(8,128)(2,1)} async-done(((bf16[1,24,512]{2,1,0:T(8,128)(2,1)}), bf16[1,1536,512]{2,1,0:T(8,128)(2,1)}) %all-gather.4.cloned.1.call-update) | async-done | bytes 1572880 | tf_op jit(solution)/shard_map/all_gather | solution.py:48
  268.0 0.0 copy-done
  268.0 0.0 copy-start.3
  268.0 0.0 copy-start.4
  268.0 11.8 %fusion.6 = f32[1536,192,16]{0,1,2:T(8,128)} fusion(bf16[192,16,512]{2,1,0:T(8,128)(2,1)S(1)} %bitcast.37, bf16[1,1536,512]{2,1,0:T(8,128)(2,1)} %all-gather.4.cloned.1.call-done), kind=kOutput, calls=%fused_computation.8 | convolution fusion | flops 4831838208 | bytes 23592960 | tf_op jit(solution)/shard_map/rhc,nc->hrn/dot_general | solution.py:18
  279.8 0.0 copy-done.3
  279.8 0.0 copy-done.4
  279.8 12.3 %fusion.17 = (f32[16,192]{1,0:T(8,128)S(1)}, f32[16,192,1536]{2,1,0:T(8,128)}) fusion(f32[1536,192,16]{0,1,2:T(8,128)} %fusion.6, bf16[192,16,64]{0,2,1:T(8,128)(2,1)S(1)} %bitcast.39, bf16[1,1536,64]{2,1,0:T(8,128)(2,1)S(1)} %all-gather.1, pred[192,1536]{1,0:T(8,128)(4,1)S(1)} %copy-done.4), kind=kOutput, calls=%fused_computation.25 | convolution fusion | flops 622851072 | bytes 38645760 | tf_op jit(solution)/shard_map/rhc,nc->hrn/dot_general | solution.py:19
  292.1 9.1 %fusion = f32[16,192]{1,0:T(8,128)S(1)} fusion(f32[16,192,1536]{2,1,0:T(8,128)} %get-tuple-element.11, f32[16,192]{1,0:T(8,128)S(1)} %get-tuple-element.10), kind=kLoop, calls=%fused_computation.2 | loop fusion | flops 9434112 | bytes 18898944 | tf_op jit(solution)/shard_map/reduce_sum | solution.py:31
  301.1 0.0 copy-start.2
  301.2 10.2 %fusion.5 = bf16[192,16,512]{2,0,1:T(8,128)(2,1)S(1)} fusion(f32[192,16]{0,1:T(8,128)S(1)} %bitcast.41, f32[16,192,1536]{2,1,0:T(8,128)} %get-tuple-element.11, f32[16,192]{1,0:T(8,128)S(1)} %get-tuple-element.10, bf16[1,1536,512]{2,1,0:T(8,128)(2,1)} %all-gather.4.cloned.1.call-done), kind=kOutput, calls=%fused_computation.7 | convolution fusion | flops 4844421120 | bytes 23617536 | tf_op jit(solution)/shard_map/hrn,nc->rhc/dot_general | solution.py:32
  311.4 0.0 copy-start.1
  311.4 1.7 copy-done.1
  313.0 0.0 copy-done.2
  313.0 3.3 convolution_bitcast_fusion
  316.4 0.0 reduce-scatter.2.cloned.1.call-update
  316.4 3.5 fusion.12
  319.9 1.4 copy.30
  321.3 2.1 reshape.103
  323.5 158.1 %reduce-scatter.2.cloned.1.call-done = f32[16,16,128]{2,0,1:T(8,128)} async-done(((f32[512,16,128]{2,0,1:T(8,128)}), f32[16,16,128]{2,0,1:T(8,128)}) %reduce-scatter.2.cloned.1.call-update) | async-done | bytes 131088 | tf_op jit(solution)/shard_map/reduce_scatter | solution.py:59
  481.5 1.6 copy.32
  (1 shorter events, 0.0 us)
Async XLA Ops:
  7.2 260.8 %copy-start = (bf16[1,192,16,512]{3,2,1,0:T(8,128)(2,1)S(1)}, bf16[1,192,16,512]{3,2,1,0:T(8,128)(2,1)}, u32[]{:S(2)}) copy-start(bf16[1,192,16,512]{3,2,1,0:T(8,128)(2,1)} %param.8) | copy-start | bytes 9437188
  7.2 260.8 %all-gather.4.cloned.1.call-start = ((), (), s32[]{:S(2)}) async-start(), calls=%async_computation.2 | async-start | bytes 1597440 | tf_op jit(solution)/shard_map/all_gather | solution.py:48
  7.9 473.6 %reduce-scatter.2.cloned.1.call-start = ((), (), s32[]{:S(2)}) async-start(), calls=%async_computation.1 | async-start | bytes 4325376 | tf_op jit(solution)/shard_map/reduce_scatter | solution.py:59
  268.0 11.8 %copy-start.3 = (bf16[1,192,1024]{1,2,0:T(8,128)(2,1)S(1)}, bf16[1,192,1024]{1,2,0:T(8,128)(2,1)}, u32[]{:S(2)}) copy-start(bf16[1,192,1024]{1,2,0:T(8,128)(2,1)} %copy.29) | copy-start | bytes 1179652
  268.0 11.8 %copy-start.4 = (pred[192,1536]{1,0:T(8,128)(4,1)S(1)}, pred[192,1536]{1,0:T(8,128)(4,1)}, u32[]{:S(2)}) copy-start(pred[192,1536]{1,0:T(8,128)(4,1)} %fusion.13) | copy-start | bytes 884740
  301.1 11.9 %copy-start.2 = (bf16[24,8,16,128]{3,2,1,0:T(8,128)(2,1)S(1)}, bf16[24,8,16,128]{3,2,1,0:T(8,128)(2,1)}, u32[]{:S(2)}) copy-start(bf16[24,8,16,128]{3,2,1,0:T(8,128)(2,1)} %copy.33) | copy-start | bytes 2359300
  311.4 1.7 copy-start.1
Sparse Core Ops, SparseCore 0:
  9.8 258.1 all-gather.3
  316.5 164.9 reduce-scatter.1
where the time goes:
time: 494 us; the launch traced here: 490 us
  waiting for transfers between devices  275 us (56%)
  blocking collectives  136 us (28%)
  matrix products  41.1 us (8%)
  between operations  14.1 us (3%)
  other arithmetic  12.1 us (2%)
  local copies, waits for them, and re-layouts  11.2 us (2%)
    reduce_scatter x1, waiting for transfers between devices, on_device(): lax.psum_scatter(jnp.einsum('rhc,rhv->chv', mixed, grads_out, preferred_e...  158 us
    all_gather x1, blocking collectives, on_device(): lax.all_gather(k_rope[0], ('ctx', 'tp'), axis=0, tiled=True)  136 us
    all_gather x1, waiting for transfers between devices, on_device(): lax.all_gather(latent[0], ('ctx', 'tp'), axis=0, tiled=True)  117 us
    dot_general x1, matrix products, attend(): jnp.einsum('rhc,nc->hrn', query_rope.reshape(count, heads, rotary), key_r...  12.3 us
    dot_general x1, matrix products, attend(): jnp.einsum('rhc,nc->hrn', query_lat, key_lat, preferred_element_type=jnp....  11.8 us
    dot_general x1, matrix products, attend(): jnp.einsum('hrn,nc->rhc', probs.astype(jnp.bfloat16), key_lat, preferred_...  10.2 us
  transfers between devices with their start and end apart: 2, of which 2 were waited for; matrix products, arithmetic and copies ran while one was open for 3% of the time, Pallas kernels for 0%

commit v1 on v0

v1 whole, which is shorter than its diff:
```python
import math
import jax
import jax.numpy as jnp
from jax import lax
from jax.experimental import pallas as pl
from jax.experimental.pallas import tpu as pltpu
from jax.sharding import PartitionSpec as P

MESH = pl.DeviceIdType.MESH
NG = 4

class Gather:
    def __init__(self, keys, send, recv):
        self.keys, self.send, self.recv = keys, send, recv
        self.z = lax.axis_index("ctx")
        tp = lax.axis_index("tp")
        self.y, self.x = tp // 4, tp % 4
        self.yp = lax.axis_index("dp") % 2
        self.yq = 1 - self.yp

    def X(self, d): return (self.x + d + 4) % 4
    def Z(self, d): return (self.z + d + 8) % 8

    def to(self, slot):
        if slot < 8: return {"tp": ((self.y + slot // 4) % 2) * 4 + self.X(slot % 4)}
        return {"ctx": self.Z(slot - 7)}

    def copy(self, z, y, x, slot):
        i = (z * 2 + y) * 4 + x
        r = self.keys.at[pl.ds(i * 3, 3)]
        return pltpu.make_async_remote_copy(src_ref=r, dst_ref=r, send_sem=self.send.at[slot, i], recv_sem=self.recv.at[i], device_id=self.to(slot), device_id_type=MESH)

    def put(self, z, y, x, slots):
        for s in slots: self.copy(z, y, x, s).start()

    def arrive(self, z, y, x):
        self.copy(z, y, x, 1).wait_recv()

    def sent(self, z, y, x, slots):
        for s in slots: self.copy(z, y, x, s).wait_send()

    def barrier(self):
        b = pltpu.get_barrier_semaphore()
        for s in range(1, 15):
            pl.semaphore_signal(b, inc=1, device_id=self.to(s), device_id_type=MESH)
        pl.semaphore_wait(b, 14)

    PLANE = (4, 1, 3, 5, 7, 2, 6)
    LINE = (8, 14, 9, 13, 10, 12, 11)
    UP, DOWN = 8, 14

    def run(self):
        x, y, z, yp, yq = self.x, self.y, self.z, self.yp, self.yq
        @pl.when(y == yp)
        def _():
            self.put(z, yp, x, (self.UP, self.DOWN) + self.PLANE)
        @pl.when(y == yq)
        def _():
            self.put(z, yq, x, self.LINE)
            self.put(z, yq, x, self.PLANE)
            self.arrive(z, yp, x)
            self.put(z, yp, x, (self.UP, self.DOWN))
        for dx in (1, 3, 2):
            self.arrive(z, yp, self.X(dx))
            self.put(z, yp, self.X(dx), (self.UP, self.DOWN))
        for d in (1, 2, 3, 4):
            for k, dx in enumerate((0, 1, 3, 2)):
                for s, zz in ((self.UP, self.Z(-d)), (self.DOWN, self.Z(d))):
                    mine = s == (self.UP, self.DOWN)[k % 2]
                    if d == 4 and not mine: continue
                    self.arrive(zz, yp, self.X(dx))
                    if d < 3 or (d == 3 and mine): self.put(zz, yp, self.X(dx), (s,))
            if d < 3:
                @pl.when(y == yq)
                def _():
                    for dz in ((1, -1, 2, -2), (3, -3, 4))[d - 1]:
                        self.arrive(self.Z(dz), yq, x)
                        self.put(self.Z(dz), yq, x, self.PLANE)
        @pl.when(y == yp)
        def _():
            for dz in (0, 1, -1, 2, -2, 3, -3, 4): self.arrive(self.Z(dz), yq, x)
        for dz in (0, 1, -1, 2, -2, 3, -3, 4):
            for dx in (1, 3, 2): self.arrive(self.Z(dz), yq, self.X(dx))

    def drain(self):
        x, y, z, yp, yq = self.x, self.y, self.z, self.yp, self.yq
        @pl.when(y == yp)
        def _():
            self.sent(z, yp, x, self.PLANE)
        @pl.when(y == yq)
        def _():
            self.sent(z, yq, x, self.LINE)
            for dz in range(8): self.sent(dz, yq, x, self.PLANE)
        for k, dx in enumerate((0, 1, 3, 2)):
            self.sent(z, yp, self.X(dx), (self.UP, self.DOWN))
            for d in (1, 2, 3):
                for s, zz in ((self.UP, self.Z(-d)), (self.DOWN, self.Z(d))):
                    mine = s == (self.UP, self.DOWN)[k % 2]
                    if d < 3 or mine: self.sent(zz, yp, self.X(dx), (s,))

def gather_kernel(lat, rope, out, keys, send, recv):
    g = Gather(keys, send, recv)
    i = (g.z * 2 + g.y) * 4 + g.x
    r = jnp.concatenate([rope[0], rope[0]], axis=1)
    for t in range(3):
        keys[i * 3 + t, :, 0:512] = lat[0, t*8:(t+1)*8, :]
        keys[i * 3 + t, :, 512:640] = r[t*8:(t+1)*8, :]
    g.barrier()
    g.run()
    g.drain()
    out[...] = keys[...]

def gather(lat, rope):
    V=pl.BlockSpec(memory_space=pltpu.VMEM)
    return pl.pallas_call(gather_kernel, out_shape=jax.ShapeDtypeStruct((192, 8, 640), jnp.bfloat16), in_specs=[V, V], out_specs=V,
        scratch_shapes=[pltpu.VMEM((192, 8, 640), jnp.bfloat16), pltpu.SemaphoreType.DMA((15, 64)), pltpu.SemaphoreType.DMA((64,))],
        compiler_params=pltpu.CompilerParams(collective_id=0, has_side_effects=True, vmem_limit_bytes=50<<20), name="gather")(lat, rope)

BLOCK=64; SPAN=448; GH=4
SCALE = 192.0 ** -0.5 * math.log2(math.e)

def start_of_doc(pos, dl):
    end = jnp.int32(0); lo = jnp.zeros_like(pos)
    for d in range(8):
        n = dl[0, d]; end = end + n
        lo = lo + jnp.where(pos >= end, n, 0)
    return lo

def compute_kernel(bo, dl, q_ref, qr_ref, do_ref, w_ref, k_ref, attn_ref, grad_ref, qt, bias, u):
    place = lax.axis_index("ctx")
    keys = k_ref.reshape(1536, 640)
    lane = lax.broadcasted_iota(jnp.int32, (64, 128), 1)
    for b in range(3):
        for c in range(4):
            x = q_ref[0, b*64:(b+1)*64, :, c*128:(c+1)*128]
            qt[b, :, :, c*128:(c+1)*128] = jnp.swapaxes(x, 0, 1)
        for j in range(8):
            pair = qr_ref[0, b*64:(b+1)*64, j*128:(j+1)*128]
            z = jnp.zeros_like(pair)
            qt[b, 2*j, :, 512:640] = jnp.where(lane < 64, pair, z)
            qt[b, 2*j+1, :, 512:640] = jnp.where(lane < 64, z, pair)
    firsts=[]
    for b in range(3):
        blk = bo[0, place*3+b]
        first = jnp.maximum(blk-6, 0)*64
        firsts.append(pl.multiple_of(first, 64))
        p = blk*64 + lax.broadcasted_iota(jnp.int32, (64, 1), 0)
        lo = start_of_doc(p, dl)
        j = first + lax.broadcasted_iota(jnp.int32, (64, SPAN), 1)
        bias[b] = jnp.where((j >= lo) & (j <= p), 0.0, -1e30)
    def group(g, _):
        for b in range(3):
            q = qt[b, pl.ds(g*GH, GH)].reshape(GH*64, 640)
            k = keys[pl.ds(firsts[b], SPAN), :]
            s = lax.dot_general(q, k, (((1,),(1,)),((),())), preferred_element_type=jnp.float32)
            s = s.reshape(GH, 64, SPAN) + bias[b][None]
            m = jnp.max(s, axis=2, keepdims=True)
            p = jnp.exp2((s - m) * SCALE)
            t = jnp.sum(p, axis=2, keepdims=True)
            pb = p.astype(jnp.bfloat16).reshape(GH*64, SPAN)
            mixed = lax.dot_general(pb, k[:, :512], (((1,),(0,)),((),())), preferred_element_type=jnp.float32)
            u[:, b*64:(b+1)*64, :] = (mixed.reshape(GH, 64, 512) / t).astype(jnp.bfloat16)
        for i in range(GH):
            h = g*GH+i
            uh = u[i]
            col = pl.ds(pl.multiple_of(h*128, 128), 128)
            attn_ref[0, :, col] = jnp.dot(uh, w_ref[h], preferred_element_type=jnp.float32).astype(jnp.bfloat16)
            gr = lax.dot_general(uh, do_ref[0, :, col], (((0,),(0,)),((),())), preferred_element_type=jnp.float32)
            grad_ref[h] = gr
        return 0
    lax.fori_loop(0, 16//GH, group, 0)

def compute(bo, dl, q, qr, do, w, k):
    V=pl.BlockSpec(memory_space=pltpu.VMEM); S=pl.BlockSpec(memory_space=pltpu.SMEM)
    return pl.pallas_call(compute_kernel,
      out_shape=[jax.ShapeDtypeStruct((1,192,2048), jnp.bfloat16), jax.ShapeDtypeStruct((16,512,128), jnp.float32)],
      in_specs=[S,S,V,V,V,V,V], out_specs=[V,V],
      scratch_shapes=[pltpu.VMEM((3,16,64,640),jnp.bfloat16), pltpu.VMEM((3,64,SPAN),jnp.float32), pltpu.VMEM((GH,192,512),jnp.bfloat16)],
      compiler_params=pltpu.CompilerParams(vmem_limit_bytes=50<<20), name="compute")(bo, dl, q, qr, do, w, k)

class Reduce:
    def __init__(self, grad, cs, cr, ys, yr, zs, zr, own, fin, sems):
        self.grad, self.cs, self.cr, self.ys, self.yr, self.zs, self.zr, self.own, self.fin = grad, cs, cr, ys, yr, zs, zr, own, fin
        self.csem, self.ysem, self.zssem, self.zrsem = sems
        self.z = lax.axis_index("ctx")
        dp = lax.axis_index("dp")
        self.hi, self.core = dp // 2, dp % 2

    def Z(self, d): return (self.z + d + 8) % 8
    def sibling(self): return {"dp": self.hi * 2 + 1 - self.core}
    def across(self): return {"dp": (1 - self.hi) * 2 + self.core}

    def targets(self):
        return [self.sibling(), self.across()] + [{"ctx": self.Z(d)} for d in range(1, 8)]

    def c_copy(self, g):
        return pltpu.make_async_remote_copy(src_ref=self.cs.at[g], dst_ref=self.cr.at[g], send_sem=self.csem.at[0, g], recv_sem=self.csem.at[1, g], device_id=self.sibling(), device_id_type=MESH)
    def y_copy(self, g):
        return pltpu.make_async_remote_copy(src_ref=self.ys.at[g], dst_ref=self.yr.at[g], send_sem=self.ysem.at[0, g], recv_sem=self.ysem.at[1, g], device_id=self.across(), device_id_type=MESH)
    def z_copy(self, g, d):
        return pltpu.make_async_remote_copy(src_ref=self.zs.at[g, self.Z(d)], dst_ref=self.zr.at[g, d - 1], send_sem=self.zssem.at[g, d - 1], recv_sem=self.zrsem.at[g, d - 1], device_id={"ctx": self.Z(d)}, device_id_type=MESH)

    def rows(self, g, i, hi, core):
        start = pl.multiple_of((hi * 2 + core) * 128, 128)
        return self.grad[g * GH + i, pl.ds(start, 128), :].reshape(8, 16, 128)

    def a(self, g):
        for hi in range(2):
            for i in range(GH):
                self.cs[g, hi, :, i] = self.rows(g, i, hi, 1 - self.core).astype(jnp.bfloat16)
        self.c_copy(g).start()

    def b(self, g):
        self.c_copy(g).wait_recv()
        for i in range(GH):
            v = self.rows(g, i, 1 - self.hi, self.core) + self.cr[g, 1 - self.hi, :, i].astype(jnp.float32)
            self.ys[g, :, i] = v.astype(jnp.bfloat16)
        self.y_copy(g).start()
        for i in range(GH):
            self.own[g, :, i] = self.rows(g, i, self.hi, self.core) + self.cr[g, self.hi, :, i].astype(jnp.float32)

    def c(self, g):
        self.y_copy(g).wait_recv()
        v = self.own[g] + self.yr[g].astype(jnp.float32)
        self.own[g] = v
        self.zs[g] = v.astype(jnp.bfloat16)
        for d in (4, 3, 5, 2, 6, 1, 7): self.z_copy(g, d).start()

    def d(self, g):
        total = self.own[g, self.z]
        for d in (1, 7, 2, 6, 3, 5, 4):
            self.z_copy(g, d).wait_recv()
            total = total + self.zr[g, d - 1].astype(jnp.float32)
        self.fin[pl.ds(g * GH, GH)] = total

    def drain(self):
        for g in range(NG):
            self.c_copy(g).wait_send(); self.y_copy(g).wait_send()
            for d in range(1, 8): self.z_copy(g, d).wait_send()

    def scratch():
        return [pltpu.VMEM((NG, 2, 8, GH, 16, 128), jnp.bfloat16), pltpu.VMEM((NG, 2, 8, GH, 16, 128), jnp.bfloat16),
          pltpu.VMEM((NG, 8, GH, 16, 128), jnp.bfloat16), pltpu.VMEM((NG, 8, GH, 16, 128), jnp.bfloat16),
          pltpu.VMEM((NG, 8, GH, 16, 128), jnp.bfloat16), pltpu.VMEM((NG, 7, GH, 16, 128), jnp.bfloat16),
          pltpu.VMEM((NG, 8, GH, 16, 128), jnp.float32), pltpu.VMEM((16, 16, 128), jnp.float32),
          pltpu.SemaphoreType.DMA((2, NG)), pltpu.SemaphoreType.DMA((2, NG)), pltpu.SemaphoreType.DMA((NG, 7)), pltpu.SemaphoreType.DMA((NG, 7))]

def reduce_kernel(grad, out, *s):
    r = Reduce(grad, *s[:8], s[8:])
    b = pltpu.get_barrier_semaphore()
    for t in r.targets(): pl.semaphore_signal(b, inc=1, device_id=t, device_id_type=MESH)
    pl.semaphore_wait(b, 9)
    stages = (r.a, r.b, r.c, r.d)
    for t in range(NG + 3):
        for k in (3, 2, 1, 0):
            if 0 <= t - k < NG: stages[k](t - k)
    r.drain()
    out[...] = jnp.swapaxes(r.fin[...], 0, 1)

def reduce(grad):
    V=pl.BlockSpec(memory_space=pltpu.VMEM)
    return pl.pallas_call(reduce_kernel, out_shape=jax.ShapeDtypeStruct((16, 16, 128), jnp.float32), in_specs=[V], out_specs=V,
        scratch_shapes=Reduce.scratch(),
        compiler_params=pltpu.CompilerParams(collective_id=1, has_side_effects=True, vmem_limit_bytes=50<<20), name="reduce")(grad)


def on_device(q_lat, q_rope, latent, k_rope, d_out, w_uv, doc_lengths, block_order):
    keys = gather(latent, k_rope)
    attn, grad = compute(block_order, doc_lengths, q_lat, q_rope, d_out, w_uv, keys)
    return attn, reduce(grad)


def solution(mesh):
    return jax.shard_map(
        on_device,
        mesh=mesh,
        in_specs=(
            P("dp", "ctx", "tp", None),
            P("dp", "ctx", "tp"),
            P("dp", ("ctx", "tp"), None),
            P("dp", ("ctx", "tp"), None),
            P("dp", "ctx", "tp"),
            P("tp", None, None),
            P("dp", None),
            P("dp", None),
        ),
        out_specs=(P("dp", "ctx", "tp"), P(("dp", "ctx"), "tp", None)),
        check_vma=False,
    )
```

time: 494 us -> 96.5 us (0.20)
  waiting for transfers between devices: 275 us -> 0 us
  blocking collectives: 136 us -> 0 us
  Pallas kernels: 0 us -> 90 us
  matrix products: 41.1 us -> 0 us
  between operations: 14.1 us -> 0.67 us
  other arithmetic: 12.1 us -> 0 us
  local copies, waits for them, and re-layouts: 11.2 us -> 5.51 us
    reduce_scatter x1 -> x0, waiting for transfers between devices: 158 us -> none  [on_device(): lax.psum_scatter(jnp.einsum('rhc,rhv->chv', mixed, grads_out, preferred_e...]
    all_gather x1 -> x0, blocking collectives: 136 us -> none  [on_device(): lax.all_gather(k_rope[0], ('ctx', 'tp'), axis=0, tiled=True)]
    all_gather x1 -> x0, waiting for transfers between devices: 117 us -> none  [on_device(): lax.all_gather(latent[0], ('ctx', 'tp'), axis=0, tiled=True)]
    pallas_call x0 -> x3, Pallas kernels: none -> 90 us  [the longest x1 37.5 us: gather(): pl.pallas_call(gather_kernel, out_shape=jax.ShapeDtypeStruct((192, 8, 640...]
    dot_general x5 -> x0, matrix products: 41.1 us -> none  [the longest x1 12.3 us: attend(): jnp.einsum('rhc,nc->hrn', query_rope.reshape(count, heads, rotary), key_r...]
    reduce_sum x3 -> x0, other arithmetic: 9.24 us -> none  [the longest x1 9.07 us: attend(): total = jnp.sum(probs, axis=2)]
  transfers between devices with their start and end apart: 2 -> 0, of which waited for: 2 -> 0; matrix products, arithmetic and copies ran while one was open for 3% -> 0% of each run, Pallas kernels for 0% -> 0%
where the time goes in v1:
time: 96.5 us; the launch traced here: 96.1 us
  Pallas kernels  90 us (93%)
  local copies, waits for them, and re-layouts  5.51 us (6%)
    pallas_call x1, Pallas kernels, gather(): pl.pallas_call(gather_kernel, out_shape=jax.ShapeDtypeStruct((192, 8, 640...  37.5 us
    pallas_call x1, Pallas kernels, reduce(): pl.pallas_call(reduce_kernel, out_shape=jax.ShapeDtypeStruct((16, 16, 128...  36.9 us
    pallas_call x1, Pallas kernels, compute(): pl.pallas_call(compute_kernel, out_shape=[jax.ShapeDtypeStruct((1, 192, 2...  15.6 us
    unnamed x13, local copies, waits for them, and re-layouts  5.51 us

profile of v1, /device:TPU:1, one launch (start us, length us, event | category | flops | bytes accessed | tf_op | source)
XLA Modules:
  0.0 96.1 jit_solution(14490118093958050606)
XLA Ops:
  0.6 0.0 copy-start.2
  0.6 0.7 copy-done.2
  1.4 0.0 copy-start.3
  1.4 0.7 copy-done.3
  2.1 37.5 %gather.1.k_ref = bf16[192,8,640]{2,1,0:T(8,128)(2,1)S(1)} custom-call(bf16[1,24,512]{2,1,0:T(8,128)(2,1)S(1)} %copy-done.2, bf16[1,24,64]{2,1,0:T(8,128)(2,1)S(1)} %copy-done.3), custom_call_target="tpu_custom_call" | custom-call | tf_op jit(solution)/shard_map/gather/pallas_call | solution.py:115
  39.6 0.0 copy-start
  39.6 1.1 %copy-done = bf16[1,192,2048]{2,1,0:T(8,128)(2,1)S(1)} copy-done((bf16[1,192,2048]{2,1,0:T(8,128)(2,1)S(1)}, bf16[1,192,2048]{2,1,0:T(8,128)(2,1)}, u32[]{:S(2)}) %copy-start) | copy-done | bytes 786456
  40.7 0.0 copy-start.1
  40.7 1.0 %copy-done.1 = bf16[1,192,1024]{2,1,0:T(8,128)(2,1)S(1)} copy-done((bf16[1,192,1024]{2,1,0:T(8,128)(2,1)S(1)}, bf16[1,192,1024]{2,1,0:T(8,128)(2,1)}, u32[]{:S(2)}) %copy-start.1) | copy-done | bytes 393240
  41.7 0.0 copy-start.4
  41.7 0.7 copy-done.4
  42.4 0.0 copy-start.5
  42.4 0.7 copy-done.5
  43.0 15.6 %compute.1 = (bf16[1,192,2048]{2,1,0:T(8,128)(2,1)}, f32[16,512,128]{2,1,0:T(8,128)}) custom-call(s32[1,24]{1,0:T(1,128)S(1)} %copy-done.4, s32[1,8]{1,0:T(1,128)S(1)} %copy-done.5, bf16[1,192,16,512]{3,2,1,0:T(8,128)(2,1)} %q_ref.1, bf16[1,192,1024]{2,1,0:T(8,128)(2,1)S(1)} %copy-done.1, bf16[1,192,2048]{2,1,0:T(8,128)(2,1)S(1)} %copy-done, ...), custom_call_target="tpu_custom_call" | custom-call | tf_op jit(solution)/shard_map/compute/pallas_call | solution.py:175
  58.6 36.9 %reduce.1 = f32[16,16,128]{2,1,0:T(8,128)S(1)} custom-call(f32[16,512,128]{2,1,0:T(8,128)} %get-tuple-element.5.grad), custom_call_target="tpu_custom_call" | custom-call | tf_op jit(solution)/shard_map/reduce/pallas_call | solution.py:262
  95.5 0.7 copy.11
Async XLA Ops:
  0.6 0.7 copy-start.2
  1.4 0.7 copy-start.3
  39.6 1.1 %copy-start = (bf16[1,192,2048]{2,1,0:T(8,128)(2,1)S(1)}, bf16[1,192,2048]{2,1,0:T(8,128)(2,1)}, u32[]{:S(2)}) copy-start(bf16[1,192,2048]{2,1,0:T(8,128)(2,1)} %do_ref.1) | copy-start | bytes 2359300
  40.7 1.0 %copy-start.1 = (bf16[1,192,1024]{2,1,0:T(8,128)(2,1)S(1)}, bf16[1,192,1024]{2,1,0:T(8,128)(2,1)}, u32[]{:S(2)}) copy-start(bf16[1,192,1024]{2,1,0:T(8,128)(2,1)} %qr_ref.1) | copy-start | bytes 1179652
  41.7 0.7 copy-start.4
  42.4 0.7 copy-start.5

commit v2 on v0

v2 whole, which is shorter than its diff:
```python
import math

import jax
import jax.numpy as jnp
from jax import lax
from jax.experimental import pallas as pl
from jax.experimental.pallas import tpu as pltpu
from jax.sharding import PartitionSpec as P

MESH = pl.DeviceIdType.MESH
BLOCK = 64
SPAN = 448
GH, NG = 4, 4
SCALE = 192.0**-0.5 * math.log2(math.e)


class Gather:
    def __init__(self, keys, send, recv):
        self.keys, self.send, self.recv = keys, send, recv
        self.z = lax.axis_index("ctx")
        tp = lax.axis_index("tp")
        self.y, self.x = tp // 4, tp % 4
        self.yp = lax.axis_index("dp") % 2
        self.yq = 1 - self.yp

    def X(self, d): return (self.x + d + 4) % 4
    def Z(self, d): return (self.z + d + 8) % 8

    def to(self, slot):
        if slot < 4: return {"tp": self.y * 4 + self.X(slot)}
        if slot == 4: return {"tp": (1 - self.y) * 4 + self.x}
        return {"ctx": self.Z(slot - 7)}

    ROW = (1, 3, 2)
    LINE = (8, 14, 9, 13, 10, 12, 11)
    UP, DOWN, UP2, DOWN2, ACROSS = 8, 14, 9, 13, 4
    Q, Q_ROW, P_LINE, P_ACROSS, COUNT = 32, 40, 41, 42, 43

    def copy(self, z, y, x, slot, arrival):
        r = self.keys.at[pl.ds(((z * 2 + y) * 4 + x) * 3, 3)]
        kind = 0 if slot < 4 else 1 if slot == 4 else 2
        return pltpu.make_async_remote_copy(src_ref=r, dst_ref=r, send_sem=self.send.at[kind], recv_sem=self.recv.at[arrival], device_id=self.to(slot), device_id_type=MESH)

    def put_p(self, z, x, slots, group=None):
        for s in slots: self.copy(z, self.yp, x, s, z * 4 + x if group is None else group).start()

    def put_q(self, z, slots, group=None):
        for s in slots: self.copy(z, self.yq, self.x, s, self.Q + z if group is None else group).start()

    def wait_p(self, z, x): self.copy(z, self.yp, x, 4, z * 4 + x).wait_recv()
    def wait_q(self, z): self.copy(z, self.yq, self.x, 4, self.Q + z).wait_recv()

    def many(self, shards, kind, arrival):
        r = self.keys.at[pl.ds(0, shards * 3)]
        return pltpu.make_async_remote_copy(src_ref=r, dst_ref=r, send_sem=self.send.at[kind], recv_sem=self.recv.at[arrival], device_id=self.to(4), device_id_type=MESH)

    def partners(self): return [self.to(s) for s in (1, 3, 2, 4) + self.LINE]

    def barrier(self):
        b = pltpu.get_barrier_semaphore()
        for t in self.partners(): pl.semaphore_signal(b, inc=1, device_id=t, device_id_type=MESH)
        pl.semaphore_wait(b, 11)

    def begin(self):
        x, z = self.x, self.z

        @pl.when(self.y == self.yp)
        def _():
            self.put_p(z, x, self.ROW)
            self.put_p(z, x, (self.ACROSS,))
            self.put_p(z, x, self.LINE, self.P_LINE)

        @pl.when(self.y == self.yq)
        def _():
            self.put_q(z, self.LINE)
            self.put_q(z, (self.ACROSS,))
            self.put_q(z, self.ROW, self.Q_ROW)

    def run(self):
        x, z = self.x, self.z
        X, Z = self.X, self.Z

        @pl.when(self.y == self.yp)
        def _():
            def near(dx):
                self.wait_p(z, X(dx))
                self.put_p(z, X(dx), (self.UP2, self.DOWN2, self.UP, self.DOWN))
                self.put_p(z, X(dx), (self.ACROSS,), self.P_ACROSS)
            def turn(dz):
                self.wait_q(Z(dz))
                self.put_q(Z(dz), self.ROW, self.Q_ROW)
            def over(dz, dx, slots=()):
                self.wait_p(Z(dz), X(dx))
                self.put_p(Z(dz), X(dx), slots)
                self.put_p(Z(dz), X(dx), (self.ACROSS,), self.P_ACROSS)
            near(1); near(3); turn(0); near(2)
            for k, dx in enumerate((1, 3, 2)):
                over(-2, dx, (self.UP, self.UP2) if k % 2 == 0 else (self.UP,))
                over(2, dx, (self.DOWN, self.DOWN2) if k % 2 == 1 else (self.DOWN,))
            turn(1); turn(-1)
            for dx in (1, 3, 2):
                over(1, dx); over(-1, dx)
            turn(2); turn(-2)
            turn(3); turn(-3); turn(4)
            for dx in (1, 3, 2):
                over(3, dx); over(-3, dx); over(4, dx)

        @pl.when(self.y == self.yq)
        def _():
            self.wait_p(z, x)
            self.put_p(z, x, self.LINE, self.P_LINE)
            for dz in (1, -1, 2, -2, 3, -3, 4):
                self.wait_q(Z(dz))
                self.put_q(Z(dz), (self.ACROSS,))
                self.put_q(Z(dz), self.ROW, self.Q_ROW)
            self.many(24, 0, self.P_ACROSS).wait_recv()

        self.many(7, 0, self.P_LINE).wait_recv()
        self.many(24, 0, self.Q_ROW).wait_recv()

    def drain(self):
        @pl.when(self.y == self.yp)
        def _():
            for kind, shards in enumerate((27, 25, 28)): self.many(shards, kind, 0).wait_send()
        @pl.when(self.y == self.yq)
        def _():
            for kind, shards in enumerate((24, 8, 14)): self.many(shards, kind, 0).wait_send()


class Reduce:
    def __init__(self, grad, cs, cr, ys, yr, zs, zr, own, fin, sems):
        self.grad, self.cs, self.cr, self.ys, self.yr, self.zs, self.zr, self.own, self.fin = grad, cs, cr, ys, yr, zs, zr, own, fin
        self.csem, self.ysem, self.zssem, self.zrsem = sems
        self.z = lax.axis_index("ctx")
        dp = lax.axis_index("dp")
        self.hi, self.core = dp // 2, dp % 2

    def Z(self, d): return (self.z + d + 8) % 8
    def sibling(self): return {"dp": self.hi * 2 + 1 - self.core}
    def across(self): return {"dp": (1 - self.hi) * 2 + self.core}

    def targets(self):
        return [self.sibling(), self.across()] + [{"ctx": self.Z(d)} for d in range(1, 8)]

    def c_copy(self, g):
        return pltpu.make_async_remote_copy(src_ref=self.cs.at[g], dst_ref=self.cr.at[g], send_sem=self.csem.at[0, g], recv_sem=self.csem.at[1, g], device_id=self.sibling(), device_id_type=MESH)
    def y_copy(self, g):
        return pltpu.make_async_remote_copy(src_ref=self.ys.at[g], dst_ref=self.yr.at[g], send_sem=self.ysem.at[0, g], recv_sem=self.ysem.at[1, g], device_id=self.across(), device_id_type=MESH)
    def z_copy(self, g, d):
        return pltpu.make_async_remote_copy(src_ref=self.zs.at[g, self.Z(d)], dst_ref=self.zr.at[g, d - 1], send_sem=self.zssem.at[g, d - 1], recv_sem=self.zrsem.at[g, d - 1], device_id={"ctx": self.Z(d)}, device_id_type=MESH)

    def rows(self, g, i, hi, core):
        start = pl.multiple_of((hi * 2 + core) * 128, 128)
        return self.grad[g * GH + i, pl.ds(start, 128), :].reshape(8, 16, 128)

    def a(self, g):
        for hi in range(2):
            for i in range(GH):
                self.cs[g, hi, :, i] = self.rows(g, i, hi, 1 - self.core).astype(jnp.bfloat16)
        self.c_copy(g).start()

    def b(self, g):
        self.c_copy(g).wait_recv()
        for i in range(GH):
            v = self.rows(g, i, 1 - self.hi, self.core) + self.cr[g, 1 - self.hi, :, i].astype(jnp.float32)
            self.ys[g, :, i] = v.astype(jnp.bfloat16)
        self.y_copy(g).start()
        for i in range(GH):
            self.own[g, :, i] = self.rows(g, i, self.hi, self.core) + self.cr[g, self.hi, :, i].astype(jnp.float32)

    def c(self, g):
        self.y_copy(g).wait_recv()
        v = self.own[g] + self.yr[g].astype(jnp.float32)
        self.own[g] = v
        self.zs[g] = v.astype(jnp.bfloat16)
        for d in (4, 3, 5, 2, 6, 1, 7): self.z_copy(g, d).start()

    def d(self, g):
        total = self.own[g, self.z]
        for d in (1, 7, 2, 6, 3, 5, 4):
            self.z_copy(g, d).wait_recv()
            total = total + self.zr[g, d - 1].astype(jnp.float32)
        self.fin[pl.ds(g * GH, GH)] = total

    def drain(self):
        for g in range(NG):
            self.c_copy(g).wait_send(); self.y_copy(g).wait_send()
            for d in range(1, 8): self.z_copy(g, d).wait_send()

    def scratch():
        return [pltpu.VMEM((NG, 2, 8, GH, 16, 128), jnp.bfloat16), pltpu.VMEM((NG, 2, 8, GH, 16, 128), jnp.bfloat16),
          pltpu.VMEM((NG, 8, GH, 16, 128), jnp.bfloat16), pltpu.VMEM((NG, 8, GH, 16, 128), jnp.bfloat16),
          pltpu.VMEM((NG, 8, GH, 16, 128), jnp.bfloat16), pltpu.VMEM((NG, 7, GH, 16, 128), jnp.bfloat16),
          pltpu.VMEM((NG, 8, GH, 16, 128), jnp.float32), pltpu.VMEM((16, 16, 128), jnp.float32),
          pltpu.SemaphoreType.DMA((2, NG)), pltpu.SemaphoreType.DMA((2, NG)), pltpu.SemaphoreType.DMA((NG, 7)), pltpu.SemaphoreType.DMA((NG, 7))]


def start_of_doc(pos, lengths):
    end, low = jnp.int32(0), jnp.zeros_like(pos)
    for d in range(8):
        n = lengths[0, d]
        end = end + n
        low = low + jnp.where(pos >= end, n, 0)
    return low


class Attend:
    def __init__(self, order, lengths, q, qr, qt, keys, bias, u):
        self.order, self.lengths, self.q, self.qr, self.qt, self.keys, self.bias, self.u = order, lengths, q, qr, qt, keys, bias, u
        self.firsts = []

    def arrange(self):
        lane = lax.broadcasted_iota(jnp.int32, (BLOCK, 128), 1)
        for b in range(3):
            rows = slice(b * BLOCK, (b + 1) * BLOCK)
            for c in range(4):
                cols = slice(c * 128, (c + 1) * 128)
                self.qt[b, :, :, cols] = jnp.swapaxes(self.q[0, rows, :, cols], 0, 1)
            for j in range(8):
                pair = self.qr[0, rows, j * 128 : (j + 1) * 128]
                zero = jnp.zeros_like(pair)
                self.qt[b, 2 * j, :, 512:640] = jnp.where(lane < 64, pair, zero)
                self.qt[b, 2 * j + 1, :, 512:640] = jnp.where(lane < 64, zero, pair)

    def mask(self):
        place = lax.axis_index("ctx")
        for b in range(3):
            block = self.order[0, place * 3 + b]
            first = jnp.maximum(block - 6, 0) * BLOCK
            self.firsts.append(jnp.maximum(block - 6, 0) * 8)
            pos = block * BLOCK + lax.broadcasted_iota(jnp.int32, (BLOCK, 1), 0)
            low = start_of_doc(pos, self.lengths)
            j = first + lax.broadcasted_iota(jnp.int32, (BLOCK, SPAN), 1)
            self.bias[b] = jnp.where((j >= low) & (j <= pos), 0.0, -1e30)

    def block(self, g, b):
        q = self.qt[b, pl.ds(g * GH, GH)].reshape(GH * BLOCK, 640)
        k = self.keys[pl.ds(self.firsts[b], SPAN // 8)].reshape(SPAN, 640)
        s = lax.dot_general(q, k, (((1,), (1,)), ((), ())), preferred_element_type=jnp.float32)
        s = s.reshape(GH, BLOCK, SPAN) + self.bias[b][None]
        top = jnp.max(s, axis=2, keepdims=True)
        p = jnp.exp2((s - top) * SCALE)
        total = jnp.sum(p, axis=2, keepdims=True)
        weights = p.astype(jnp.bfloat16).reshape(GH * BLOCK, SPAN)
        mixed = lax.dot_general(weights, k[:, :512], (((1,), (0,)), ((), ())), preferred_element_type=jnp.float32)
        self.u[pl.ds(g * GH, GH), b * BLOCK : (b + 1) * BLOCK, :] = (mixed.reshape(GH, BLOCK, 512) / total).astype(jnp.bfloat16)


def kernel(order_hbm, lengths_hbm, lat_hbm, rope_hbm, q_hbm, qr_hbm, do_hbm, w_hbm, attn, out, order, lengths, lat, rope, q, qr, do, w, loads, keys, send, recv, qt, bias, u, grad, *reduce_refs):
    copies = [
        pltpu.make_async_copy(src, dst, loads.at[i])
        for i, (src, dst) in enumerate(
            ((lat_hbm, lat), (rope_hbm, rope), (order_hbm, order), (lengths_hbm, lengths), (q_hbm, q), (qr_hbm, qr), (do_hbm, do), (w_hbm, w))
        )
    ]
    for c in copies:
        c.start()
    g = Gather(keys, send, recv)
    r = Reduce(grad, *reduce_refs[:8], reduce_refs[8:])
    barrier = pltpu.get_barrier_semaphore()
    partners = g.partners() + r.targets()[:2]
    for t in partners:
        pl.semaphore_signal(barrier, inc=1, device_id=t, device_id_type=MESH)
    copies[0].wait()
    copies[1].wait()
    mine = ((g.z * 2 + g.y) * 4 + g.x) * 3
    twice = jnp.concatenate([rope[0], rope[0]], axis=1)
    for t in range(3):
        keys[mine + t, :, 0:512] = lat[0, t * 8 : (t + 1) * 8, :]
        keys[mine + t, :, 512:640] = twice[t * 8 : (t + 1) * 8, :]
    pl.semaphore_wait(barrier, len(partners))
    g.begin()
    for c in copies[2:]:
        c.wait()
    a = Attend(order, lengths, q, qr, qt, keys, bias, u)
    a.arrange()
    a.mask()
    g.run()

    def group(i, _):
        a.block(i, 0)
        pl.when(i >= 1)(lambda: r.b(i - 1))
        a.block(i, 1)
        pl.when(i >= 2)(lambda: r.c(i - 2))
        a.block(i, 2)
        pl.when(i >= 3)(lambda: r.d(i - 3))
        for h in range(GH):
            head = i * GH + h
            col = pl.ds(pl.multiple_of(head * 128, 128), 128)
            grad[head] = lax.dot_general(u[head], do[0, :, col], (((0,), (0,)), ((), ())), preferred_element_type=jnp.float32)
        r.a(i)
        return 0

    lax.fori_loop(0, NG, group, 0)

    def values(i):
        def head(h, _):
            col = pl.ds(pl.multiple_of(h * 128, 128), 128)
            attn[0, :, col] = jnp.dot(u[h], w[h], preferred_element_type=jnp.float32).astype(jnp.bfloat16)
            return 0

        lax.fori_loop(i * GH, (i + 1) * GH, head, 0)

    values(0)
    r.b(3)
    r.c(2)
    r.d(1)
    values(1)
    values(2)
    r.c(3)
    values(3)
    r.d(2)
    r.d(3)
    out[...] = jnp.swapaxes(r.fin[...], 0, 1)
    g.drain()
    r.drain()


def on_device(q_lat, q_rope, latent, k_rope, d_out, w_uv, doc_lengths, block_order):
    hbm = pl.BlockSpec(memory_space=pltpu.HBM)
    vmem = pl.BlockSpec(memory_space=pltpu.VMEM)
    operands = (block_order, doc_lengths, latent, k_rope, q_lat, q_rope, d_out, w_uv)
    return pl.pallas_call(
        kernel,
        out_shape=[jax.ShapeDtypeStruct((1, 192, 2048), jnp.bfloat16), jax.ShapeDtypeStruct((16, 16, 128), jnp.float32)],
        in_specs=[hbm] * 8,
        out_specs=[vmem, vmem],
        scratch_shapes=[
            pltpu.SMEM((1, 24), jnp.int32),
            pltpu.SMEM((1, 8), jnp.int32),
            *(pltpu.VMEM(x.shape, x.dtype) for x in operands[2:]),
            pltpu.SemaphoreType.DMA((8,)),
            pltpu.VMEM((192, 8, 640), jnp.bfloat16),
            pltpu.SemaphoreType.DMA((3,)),
            pltpu.SemaphoreType.DMA((Gather.COUNT,)),
            pltpu.VMEM((3, 16, BLOCK, 640), jnp.bfloat16),
            pltpu.VMEM((3, BLOCK, SPAN), jnp.float32),
            pltpu.VMEM((16, 192, 512), jnp.bfloat16),
            pltpu.VMEM((16, 512, 128), jnp.float32),
            *Reduce.scratch(),
        ],
        compiler_params=pltpu.CompilerParams(collective_id=0, has_side_effects=True, vmem_limit_bytes=56 << 20),
        name="attention",
    )(*operands)


def solution(mesh):
    return jax.shard_map(
        on_device,
        mesh=mesh,
        in_specs=(
            P("dp", "ctx", "tp", None),
            P("dp", "ctx", "tp"),
            P("dp", ("ctx", "tp"), None),
            P("dp", ("ctx", "tp"), None),
            P("dp", "ctx", "tp"),
            P("tp", None, None),
            P("dp", None),
            P("dp", None),
        ),
        out_specs=(P("dp", "ctx", "tp"), P(("dp", "ctx"), "tp", None)),
        check_vma=False,
    )
```

time: 494 us -> 64 us (0.13)
  waiting for transfers between devices: 275 us -> 0 us
  blocking collectives: 136 us -> 0 us
  Pallas kernels: 0 us -> 59.5 us
  matrix products: 41.1 us -> 0 us
  between operations: 14.1 us -> 0.64 us
  other arithmetic: 12.1 us -> 0 us
  local copies, waits for them, and re-layouts: 11.2 us -> 3.66 us
    reduce_scatter x1 -> x0, waiting for transfers between devices: 158 us -> none  [on_device(): lax.psum_scatter(jnp.einsum('rhc,rhv->chv', mixed, grads_out, preferred_e...]
    all_gather x1 -> x0, blocking collectives: 136 us -> none  [on_device(): lax.all_gather(k_rope[0], ('ctx', 'tp'), axis=0, tiled=True)]
    all_gather x1 -> x0, waiting for transfers between devices: 117 us -> none  [on_device(): lax.all_gather(latent[0], ('ctx', 'tp'), axis=0, tiled=True)]
    pallas_call x0 -> x1, Pallas kernels: none -> 59.5 us  [on_device(): pl.pallas_call(kernel, out_shape=[jax.ShapeDtypeStruct((1, 192, 2048), jn...]
    dot_general x5 -> x0, matrix products: 41.1 us -> none  [the longest x1 12.3 us: attend(): jnp.einsum('rhc,nc->hrn', query_rope.reshape(count, heads, rotary), key_r...]
    reduce_sum x3 -> x0, other arithmetic: 9.24 us -> none  [the longest x1 9.07 us: attend(): total = jnp.sum(probs, axis=2)]
  transfers between devices with their start and end apart: 2 -> 0, of which waited for: 2 -> 0; matrix products, arithmetic and copies ran while one was open for 3% -> 0% of each run, Pallas kernels for 0% -> 0%
where the time goes in v2:
time: 64 us; the launch traced here: 63.8 us
  Pallas kernels  59.5 us (93%)
  local copies, waits for them, and re-layouts  3.66 us (6%)
  between operations  0.64 us (1%)
    pallas_call x1, Pallas kernels, on_device(): pl.pallas_call(kernel, out_shape=[jax.ShapeDtypeStruct((1, 192, 2048), jn...  59.5 us
    unnamed x2, local copies, waits for them, and re-layouts  3.66 us

profile of v2, /device:TPU:1, one launch (start us, length us, event | category | flops | bytes accessed | tf_op | source)
XLA Modules:
  0.0 63.8 jit_solution(4379070734678883535)
XLA Ops:
  0.6 59.5 %attention.1 = (bf16[1,192,2048]{2,1,0:T(8,128)(2,1)}, f32[16,16,128]{2,1,0:T(8,128)}) custom-call(s32[1,24]{1,0:T(1,128)} %order_hbm.1, s32[1,8]{1,0:T(1,128)} %lengths_hbm.1, bf16[1,24,512]{2,1,0:T(8,128)(2,1)} %lat_hbm.1, bf16[1,24,64]{2,1,0:T(8,128)(2,1)} %rope_hbm.1, bf16[1,192,16,512]{3,2,1,0:T(8,128)(2,1)} %q_hbm.1, bf16[1,192,1024]{2,1,0:T(8,128)(2,1)} %qr_hbm.1, ...), custom_call_target="tpu_custom_call" | custom-call | tf_op jit(solution)/shard_map/attention/pallas_call | solution.py:323
  60.1 2.1 %copy.12 = bf16[1,192,2048]{2,1,0:T(8,128)(2,1)} copy(bf16[1,192,2048]{2,1,0:T(8,128)(2,1)} %get-tuple-element.4) | data formatting | bytes 1572864
  62.2 1.6 %copy.13 = f32[16,16,128]{2,1,0:T(8,128)} copy(f32[16,16,128]{2,1,0:T(8,128)} %get-tuple-element.5) | data formatting | bytes 262144

commit v3 on v2

--- a/solution.py
+++ b/solution.py
@@ -10,7 +10,11 @@
 MESH = pl.DeviceIdType.MESH
 BLOCK = 64
 SPAN = 448
-GH, NG = 4, 4
+GH = 4
+UH, NU = 2, 8
+Z_FIRST = (0, 4)
+Y_FIRST = tuple(u for u in range(NU) if u not in Z_FIRST)
+VMEM_MB = 56
 SCALE = 192.0**-0.5 * math.log2(math.e)
 
 
@@ -128,71 +132,136 @@
 
 
 class Reduce:
-    def __init__(self, grad, cs, cr, ys, yr, zs, zr, own, fin, sems):
-        self.grad, self.cs, self.cr, self.ys, self.yr, self.zs, self.zr, self.own, self.fin = grad, cs, cr, ys, yr, zs, zr, own, fin
-        self.csem, self.ysem, self.zssem, self.zrsem = sems
+    def __init__(self, grad, fin, cs, cr, ys, yr, zs, zr, zs2, zr2, ys2, yr2, acc, sent, csem, ysem, zsem):
+        self.grad, self.fin, self.cs, self.cr, self.ys, self.yr, self.zs, self.zr = grad, fin, cs, cr, ys, yr, zs, zr
+        self.zs2, self.zr2, self.ys2, self.yr2, self.acc = zs2, zr2, ys2, yr2, acc
+        self.sem, self.csem, self.ysem, self.zsem = sent, csem, ysem, zsem
         self.z = lax.axis_index("ctx")
         dp = lax.axis_index("dp")
         self.hi, self.core = dp // 2, dp % 2
 
-    def Z(self, d): return (self.z + d + 8) % 8
-    def sibling(self): return {"dp": self.hi * 2 + 1 - self.core}
-    def across(self): return {"dp": (1 - self.hi) * 2 + self.core}
-
-    def targets(self):
-        return [self.sibling(), self.across()] + [{"ctx": self.Z(d)} for d in range(1, 8)]
-
-    def c_copy(self, g):
-        return pltpu.make_async_remote_copy(src_ref=self.cs.at[g], dst_ref=self.cr.at[g], send_sem=self.csem.at[0, g], recv_sem=self.csem.at[1, g], device_id=self.sibling(), device_id_type=MESH)
-    def y_copy(self, g):
-        return pltpu.make_async_remote_copy(src_ref=self.ys.at[g], dst_ref=self.yr.at[g], send_sem=self.ysem.at[0, g], recv_sem=self.ysem.at[1, g], device_id=self.across(), device_id_type=MESH)
-    def z_copy(self, g, d):
-        return pltpu.make_async_remote_copy(src_ref=self.zs.at[g, self.Z(d)], dst_ref=self.zr.at[g, d - 1], send_sem=self.zssem.at[g, d - 1], recv_sem=self.zrsem.at[g, d - 1], device_id={"ctx": self.Z(d)}, device_id_type=MESH)
-
-    def rows(self, g, i, hi, core):
+    FAR_FIRST = (4, 3, 5, 2, 6, 1, 7)
+
+    def Z(self, d):
+        return (self.z + d + 8) % 8
+
+    def sibling(self):
+        return {"dp": self.hi * 2 + 1 - self.core}
+
+    def across(self):
+        return {"dp": (1 - self.hi) * 2 + self.core}
+
+    def copy(self, src, dst, kind, recv, to):
+        return pltpu.make_async_remote_copy(
+            src_ref=src, dst_ref=dst, send_sem=self.sem.at[kind], recv_sem=recv, device_id=to, device_id_type=MESH
+        )
+
+    def bufs(self, u):
+        if u in Z_FIRST:
+            k = Z_FIRST.index(u)
+            return self.ys2.at[k], self.yr2.at[k], self.zs2.at[k], self.zr2.at[k]
+        k = Y_FIRST.index(u)
+        return self.ys.at[k], self.yr.at[k], self.zs.at[k], self.zr.at[k]
+
+    def c_copy(self, u):
+        return self.copy(self.cs.at[u], self.cr.at[u], 0, self.csem.at[u], self.sibling())
+
+    def y_copy(self, u):
+        ys, yr, _, _ = self.bufs(u)
+        return self.copy(ys, yr, 3 if u in Z_FIRST else 1, self.ysem.at[u], self.across())
+
+    def z_start(self, u):
+        _, _, zs, zr = self.bufs(u)
+        for d in self.FAR_FIRST:
+            self.copy(zs.at[self.Z(d)], zr.at[d - 1], 4 if u in Z_FIRST else 2, self.zsem.at[u], {"ctx": self.Z(d)}).start()
+
+    def z_wait(self, u):
+        _, _, _, zr = self.bufs(u)
+        self.copy(zr, zr, 2, self.zsem.at[u], self.across()).wait_recv()
+
+    def rows(self, u, i, hi, core):
         start = pl.multiple_of((hi * 2 + core) * 128, 128)
-        return self.grad[g * GH + i, pl.ds(start, 128), :].reshape(8, 16, 128)
-
-    def a(self, g):
+        return self.grad[u * UH + i, pl.ds(start, 128), :].reshape(8, 16, 128)
+
+    def both(self, u, i, hi):
+        return self.rows(u, i, hi, self.core) + self.cr[u, hi, :, i].astype(jnp.float32)
+
+    def mine(self, u, i, hi):
+        start = pl.multiple_of((hi * 2 + self.core) * 128 + self.z * 16, 16)
+        return self.grad[u * UH + i, pl.ds(start, 16), :] + self.cr[u, hi, self.z, i].astype(jnp.float32)
+
+    def a(self, u):
         for hi in range(2):
-            for i in range(GH):
-                self.cs[g, hi, :, i] = self.rows(g, i, hi, 1 - self.core).astype(jnp.bfloat16)
-        self.c_copy(g).start()
-
-    def b(self, g):
-        self.c_copy(g).wait_recv()
-        for i in range(GH):
-            v = self.rows(g, i, 1 - self.hi, self.core) + self.cr[g, 1 - self.hi, :, i].astype(jnp.float32)
-            self.ys[g, :, i] = v.astype(jnp.bfloat16)
-        self.y_copy(g).start()
-        for i in range(GH):
-            self.own[g, :, i] = self.rows(g, i, self.hi, self.core) + self.cr[g, self.hi, :, i].astype(jnp.float32)
-
-    def c(self, g):
-        self.y_copy(g).wait_recv()
-        v = self.own[g] + self.yr[g].astype(jnp.float32)
-        self.own[g] = v
-        self.zs[g] = v.astype(jnp.bfloat16)
-        for d in (4, 3, 5, 2, 6, 1, 7): self.z_copy(g, d).start()
-
-    def d(self, g):
-        total = self.own[g, self.z]
-        for d in (1, 7, 2, 6, 3, 5, 4):
-            self.z_copy(g, d).wait_recv()
-            total = total + self.zr[g, d - 1].astype(jnp.float32)
-        self.fin[pl.ds(g * GH, GH)] = total
+            for i in range(UH):
+                self.cs[u, hi, :, i] = self.rows(u, i, hi, 1 - self.core).astype(jnp.bfloat16)
+        self.c_copy(u).start()
+
+    def b(self, u):
+        self.c_copy(u).wait_recv()
+        ys, _, zs, _ = self.bufs(u)
+        for i in range(UH):
+            if u in Z_FIRST:
+                for hi in range(2):
+                    zs[:, hi, i] = self.both(u, i, hi).astype(jnp.bfloat16)
+            else:
+                ys[:, i] = self.both(u, i, 1 - self.hi).astype(jnp.bfloat16)
+        if u in Z_FIRST:
+            self.z_start(u)
+        else:
+            self.y_copy(u).start()
+
+    def c(self, u):
+        ys, yr, zs, zr = self.bufs(u)
+        if u in Z_FIRST:
+            self.z_wait(u)
+            k = Z_FIRST.index(u)
+            for i in range(UH):
+                for far in range(2):
+                    hi = 1 - self.hi if far else self.hi
+                    total = self.mine(u, i, hi)
+                    for d in range(7):
+                        total = total + zr[d, hi, i].astype(jnp.float32)
+                    if far:
+                        ys[i] = total.astype(jnp.bfloat16)
+                    else:
+                        self.acc[k, i] = total
+            self.y_copy(u).start()
+        else:
+            self.y_copy(u).wait_recv()
+            for i in range(UH):
+                zs[:, i] = (self.both(u, i, self.hi) + yr[:, i].astype(jnp.float32)).astype(jnp.bfloat16)
+            self.z_start(u)
+
+    def d(self, u):
+        _, yr, _, zr = self.bufs(u)
+        if u in Z_FIRST:
+            self.y_copy(u).wait_recv()
+        else:
+            self.z_wait(u)
+        for i in range(UH):
+            if u in Z_FIRST:
+                total = self.acc[Z_FIRST.index(u), i] + yr[i].astype(jnp.float32)
+            else:
+                total = self.mine(u, i, self.hi) + yr[self.z, i].astype(jnp.float32)
+                for d in range(7):
+                    total = total + zr[d, i].astype(jnp.float32)
+            self.fin[u * UH + i] = total
 
     def drain(self):
-        for g in range(NG):
-            self.c_copy(g).wait_send(); self.y_copy(g).wait_send()
-            for d in range(1, 8): self.z_copy(g, d).wait_send()
+        for kind, whole in enumerate((self.cs, self.ys, self.zr, self.ys2, self.zr2)):
+            self.copy(whole, whole, kind, self.csem.at[0], self.across()).wait_send()
 
     def scratch():
-        return [pltpu.VMEM((NG, 2, 8, GH, 16, 128), jnp.bfloat16), pltpu.VMEM((NG, 2, 8, GH, 16, 128), jnp.bfloat16),
-          pltpu.VMEM((NG, 8, GH, 16, 128), jnp.bfloat16), pltpu.VMEM((NG, 8, GH, 16, 128), jnp.bfloat16),
-          pltpu.VMEM((NG, 8, GH, 16, 128), jnp.bfloat16), pltpu.VMEM((NG, 7, GH, 16, 128), jnp.bfloat16),
-          pltpu.VMEM((NG, 8, GH, 16, 128), jnp.float32), pltpu.VMEM((16, 16, 128), jnp.float32),
-          pltpu.SemaphoreType.DMA((2, NG)), pltpu.SemaphoreType.DMA((2, NG)), pltpu.SemaphoreType.DMA((NG, 7)), pltpu.SemaphoreType.DMA((NG, 7))]
+        tile, half = (UH, 16, 128), (2, UH, 16, 128)
+        ny, nz = len(Y_FIRST), len(Z_FIRST)
+        shapes = [(NU, 2, 8) + tile] * 2 + [(ny, 8) + tile] * 3 + [(ny, 7) + tile, (nz, 8) + half, (nz, 7) + half, (nz,) + tile, (nz,) + tile]
+        return [
+            pltpu.VMEM((16, 16, 128), jnp.float32),
+            *(pltpu.VMEM(shape, jnp.bfloat16) for shape in shapes),
+            pltpu.VMEM((nz,) + tile, jnp.float32),
+            pltpu.SemaphoreType.DMA((5,)),
+            *[pltpu.SemaphoreType.DMA((NU,))] * 3,
+        ]
 
 
 def start_of_doc(pos, lengths):
@@ -233,17 +302,17 @@
             j = first + lax.broadcasted_iota(jnp.int32, (BLOCK, SPAN), 1)
             self.bias[b] = jnp.where((j >= low) & (j <= pos), 0.0, -1e30)
 
-    def block(self, g, b):
-        q = self.qt[b, pl.ds(g * GH, GH)].reshape(GH * BLOCK, 640)
+    def block(self, head, n, b):
+        q = self.qt[b, pl.ds(head, n)].reshape(n * BLOCK, 640)
         k = self.keys[pl.ds(self.firsts[b], SPAN // 8)].reshape(SPAN, 640)
         s = lax.dot_general(q, k, (((1,), (1,)), ((), ())), preferred_element_type=jnp.float32)
-        s = s.reshape(GH, BLOCK, SPAN) + self.bias[b][None]
+        s = s.reshape(n, BLOCK, SPAN) + self.bias[b][None]
         top = jnp.max(s, axis=2, keepdims=True)
         p = jnp.exp2((s - top) * SCALE)
         total = jnp.sum(p, axis=2, keepdims=True)
-        weights = p.astype(jnp.bfloat16).reshape(GH * BLOCK, SPAN)
+        weights = p.astype(jnp.bfloat16).reshape(n * BLOCK, SPAN)
         mixed = lax.dot_general(weights, k[:, :512], (((1,), (0,)), ((), ())), preferred_element_type=jnp.float32)
-        self.u[pl.ds(g * GH, GH), b * BLOCK : (b + 1) * BLOCK, :] = (mixed.reshape(GH, BLOCK, 512) / total).astype(jnp.bfloat16)
+        self.u[pl.ds(head, n), b * BLOCK : (b + 1) * BLOCK, :] = (mixed.reshape(n, BLOCK, 512) / total).astype(jnp.bfloat16)
 
 
 def kernel(order_hbm, lengths_hbm, lat_hbm, rope_hbm, q_hbm, qr_hbm, do_hbm, w_hbm, attn, out, order, lengths, lat, rope, q, qr, do, w, loads, keys, send, recv, qt, bias, u, grad, *reduce_refs):
@@ -256,9 +325,9 @@
     for c in copies:
         c.start()
     g = Gather(keys, send, recv)
-    r = Reduce(grad, *reduce_refs[:8], reduce_refs[8:])
+    r = Reduce(grad, *reduce_refs)
     barrier = pltpu.get_barrier_semaphore()
-    partners = g.partners() + r.targets()[:2]
+    partners = g.partners() + [r.sibling(), r.across()]
     for t in partners:
         pl.semaphore_signal(barrier, inc=1, device_id=t, device_id_type=MESH)
     copies[0].wait()
@@ -277,21 +346,23 @@
     a.mask()
     g.run()
 
-    def group(i, _):
-        a.block(i, 0)
-        pl.when(i >= 1)(lambda: r.b(i - 1))
-        a.block(i, 1)
-        pl.when(i >= 2)(lambda: r.c(i - 2))
-        a.block(i, 2)
-        pl.when(i >= 3)(lambda: r.d(i - 3))
-        for h in range(GH):
-            head = i * GH + h
-            col = pl.ds(pl.multiple_of(head * 128, 128), 128)
-            grad[head] = lax.dot_general(u[head], do[0, :, col], (((0,), (0,)), ((), ())), preferred_element_type=jnp.float32)
-        r.a(i)
-        return 0
-
-    lax.fori_loop(0, NG, group, 0)
+    def gradient(first, n):
+        for h in range(n):
+            col = pl.ds(pl.multiple_of((first + h) * 128, 128), 128)
+            grad[first + h] = lax.dot_general(u[first + h], do[0, :, col], (((0,), (0,)), ((), ())), preferred_element_type=jnp.float32)
+
+    def group(first, n, work, units):
+        for b in range(3):
+            a.block(first, n, b)
+            for act, u in work[b]:
+                act(u)
+        gradient(first, n)
+        for u in units:
+            r.a(u)
+
+    none = ()
+    group(0, 8, (none, none, none), (2, 0, 3, 1))
+    group(8, 8, (((r.b, 2), (r.b, 0), (r.b, 3), (r.b, 1)), none, none), (5, 4, 6, 7))
 
     def values(i):
         def head(h, _):
@@ -302,15 +373,19 @@
         lax.fori_loop(i * GH, (i + 1) * GH, head, 0)
 
     values(0)
-    r.b(3)
-    r.c(2)
-    r.d(1)
+    for unit in (5, 4, 6, 7):
+        r.b(unit)
+    for unit in (2, 3):
+        r.c(unit)
     values(1)
+    for unit in (5, 0, 1):
+        r.c(unit)
     values(2)
-    r.c(3)
+    for unit in (6, 7, 4):
+        r.c(unit)
     values(3)
-    r.d(2)
-    r.d(3)
+    for unit in (2, 3, 5, 0, 1, 6, 4, 7):
+        r.d(unit)
     out[...] = jnp.swapaxes(r.fin[...], 0, 1)
     g.drain()
     r.drain()
@@ -322,7 +397,7 @@
     operands = (block_order, doc_lengths, latent, k_rope, q_lat, q_rope, d_out, w_uv)
     return pl.pallas_call(
         kernel,
-        out_shape=[jax.ShapeDtypeStruct((1, 192, 2048), jnp.bfloat16), jax.ShapeDtypeStruct((16, 16, 128), jnp.float32)],
+        out_shape=[pltpu.VMEM((1, 192, 2048), jnp.bfloat16), pltpu.VMEM((16, 16, 128), jnp.float32)],
         in_specs=[hbm] * 8,
         out_specs=[vmem, vmem],
         scratch_shapes=[
@@ -339,7 +414,7 @@
             pltpu.VMEM((16, 512, 128), jnp.float32),
             *Reduce.scratch(),
         ],
-        compiler_params=pltpu.CompilerParams(collective_id=0, has_side_effects=True, vmem_limit_bytes=56 << 20),
+        compiler_params=pltpu.CompilerParams(collective_id=0, has_side_effects=True, vmem_limit_bytes=VMEM_MB << 20),
         name="attention",
     )(*operands)
 

time: 64 us -> 55.6 us (0.87)
  Pallas kernels: 59.5 us -> 52.7 us
  local copies, waits for them, and re-layouts: 3.66 us -> 1.54 us
    pallas_call x1, Pallas kernels: 59.5 us -> 52.7 us  [on_device(): pl.pallas_call(kernel, out_shape=[pltpu.VMEM((1, 192, 2048), jnp.bfloat16...]
    unnamed x2, local copies, waits for them, and re-layouts: 3.66 us -> 1.54 us
where the time goes in v3:
time: 55.6 us; the launch traced here: 54.9 us
  Pallas kernels  52.7 us (95%)
  local copies, waits for them, and re-layouts  1.54 us (3%)
  between operations  0.64 us (1%)
    pallas_call x1, Pallas kernels, on_device(): pl.pallas_call(kernel, out_shape=[pltpu.VMEM((1, 192, 2048), jnp.bfloat16...  52.7 us
    unnamed x2, local copies, waits for them, and re-layouts  1.54 us

profile of v3, /device:TPU:1, one launch (start us, length us, event | category | flops | bytes accessed | tf_op | source)
XLA Modules:
  0.0 54.9 jit_solution(14617481439971814752)
XLA Ops:
  0.6 52.7 %attention.1 = (bf16[1,192,2048]{2,1,0:T(8,128)(2,1)S(1)}, f32[16,16,128]{2,1,0:T(8,128)S(1)}) custom-call(s32[1,24]{1,0:T(1,128)} %order_hbm.1, s32[1,8]{1,0:T(1,128)} %lengths_hbm.1, bf16[1,24,512]{2,1,0:T(8,128)(2,1)} %lat_hbm.1, bf16[1,24,64]{2,1,0:T(8,128)(2,1)} %rope_hbm.1, bf16[1,192,16,512]{3,2,1,0:T(8,128)(2,1)} %q_hbm.1, ...), custom_call_target="tpu_custom_call" | custom-call | tf_op jit(solution)/shard_map/attention/pallas_call | solution.py:398
  53.4 0.9 %copy.12 = bf16[1,192,2048]{2,1,0:T(8,128)(2,1)} copy(bf16[1,192,2048]{2,1,0:T(8,128)(2,1)S(1)} %get-tuple-element.2) | data formatting | bytes 1572864
  54.2 0.7 %copy.13 = f32[16,16,128]{2,1,0:T(8,128)} copy(f32[16,16,128]{2,1,0:T(8,128)S(1)} %get-tuple-element.3) | data formatting | bytes 262144

commit v4 on v3

--- a/solution.py
+++ b/solution.py
@@ -12,7 +12,7 @@
 SPAN = 448
 GH = 4
 UH, NU = 2, 8
-Z_FIRST = (0, 4)
+Z_FIRST = (0, 3)
 Y_FIRST = tuple(u for u in range(NU) if u not in Z_FIRST)
 VMEM_MB = 56
 SCALE = 192.0**-0.5 * math.log2(math.e)
@@ -72,7 +72,8 @@
         def _():
             self.put_p(z, x, self.ROW)
             self.put_p(z, x, (self.ACROSS,))
-            self.put_p(z, x, self.LINE, self.P_LINE)
+            self.put_p(z, x, (self.UP2, self.DOWN2))
+            self.put_p(z, x, (self.UP, self.DOWN), self.P_LINE)
 
         @pl.when(self.y == self.yq)
         def _():
@@ -83,6 +84,12 @@
     def run(self):
         x, z = self.x, self.z
         X, Z = self.X, self.Z
+
+        def hop(up, down):
+            self.wait_p(Z(-2), x)
+            self.put_p(Z(-2), x, up, self.P_LINE)
+            self.wait_p(Z(2), x)
+            self.put_p(Z(2), x, down, self.P_LINE)
 
         @pl.when(self.y == self.yp)
         def _():
@@ -97,29 +104,36 @@
                 self.wait_p(Z(dz), X(dx))
                 self.put_p(Z(dz), X(dx), slots)
                 self.put_p(Z(dz), X(dx), (self.ACROSS,), self.P_ACROSS)
-            near(1); near(3); turn(0); near(2)
-            for k, dx in enumerate((1, 3, 2)):
-                over(-2, dx, (self.UP, self.UP2) if k % 2 == 0 else (self.UP,))
-                over(2, dx, (self.DOWN, self.DOWN2) if k % 2 == 1 else (self.DOWN,))
-            turn(1); turn(-1)
+            near(1); near(3); near(2)
+            hop((self.UP, self.UP2), (self.DOWN,))
+            turn(0); turn(1); turn(-1)
+            over(-2, 1, (self.UP, self.UP2)); over(2, 1, (self.DOWN,))
+            over(-2, 3, (self.UP,)); over(2, 3, (self.DOWN, self.DOWN2))
+            turn(2); turn(-2)
+            over(-2, 2, (self.UP, self.UP2)); over(2, 2, (self.DOWN,))
             for dx in (1, 3, 2):
                 over(1, dx); over(-1, dx)
-            turn(2); turn(-2)
             turn(3); turn(-3); turn(4)
             for dx in (1, 3, 2):
                 over(3, dx); over(-3, dx); over(4, dx)
 
         @pl.when(self.y == self.yq)
         def _():
-            self.wait_p(z, x)
-            self.put_p(z, x, self.LINE, self.P_LINE)
-            for dz in (1, -1, 2, -2, 3, -3, 4):
+            def cross(dz):
                 self.wait_q(Z(dz))
                 self.put_q(Z(dz), (self.ACROSS,))
                 self.put_q(Z(dz), self.ROW, self.Q_ROW)
+            for dz in (1, -1, 2, -2):
+                cross(dz)
+            self.wait_p(z, x)
+            self.put_p(z, x, (self.UP2, self.DOWN2))
+            self.put_p(z, x, (self.UP, self.DOWN), self.P_LINE)
+            for dz in (3, -3, 4):
+                cross(dz)
+            hop((self.UP,), (self.DOWN, self.DOWN2))
             self.many(24, 0, self.P_ACROSS).wait_recv()
 
-        self.many(7, 0, self.P_LINE).wait_recv()
+        self.many(5, 0, self.P_LINE).wait_recv()
         self.many(24, 0, self.Q_ROW).wait_recv()
 
     def drain(self):
@@ -322,14 +336,14 @@
             ((lat_hbm, lat), (rope_hbm, rope), (order_hbm, order), (lengths_hbm, lengths), (q_hbm, q), (qr_hbm, qr), (do_hbm, do), (w_hbm, w))
         )
     ]
-    for c in copies:
-        c.start()
     g = Gather(keys, send, recv)
     r = Reduce(grad, *reduce_refs)
     barrier = pltpu.get_barrier_semaphore()
     partners = g.partners() + [r.sibling(), r.across()]
     for t in partners:
         pl.semaphore_signal(barrier, inc=1, device_id=t, device_id_type=MESH)
+    for c in copies:
+        c.start()
     copies[0].wait()
     copies[1].wait()
     mine = ((g.z * 2 + g.y) * 4 + g.x) * 3
@@ -361,8 +375,9 @@
             r.a(u)
 
     none = ()
-    group(0, 8, (none, none, none), (2, 0, 3, 1))
-    group(8, 8, (((r.b, 2), (r.b, 0), (r.b, 3), (r.b, 1)), none, none), (5, 4, 6, 7))
+    group(0, 6, (none, none, none), (1, 0, 2))
+    group(6, 6, (((r.b, 1), (r.b, 0), (r.b, 2)), none, none), (4, 3, 5))
+    group(12, 4, (none, ((r.b, 4), (r.b, 3), (r.b, 5)), none), (6, 7))
 
     def values(i):
         def head(h, _):
@@ -373,18 +388,18 @@
         lax.fori_loop(i * GH, (i + 1) * GH, head, 0)
 
     values(0)
-    for unit in (5, 4, 6, 7):
+    for unit in (6, 7):
         r.b(unit)
-    for unit in (2, 3):
+    for unit in (1, 2):
         r.c(unit)
     values(1)
-    for unit in (5, 0, 1):
+    for unit in (0, 4, 5):
         r.c(unit)
     values(2)
-    for unit in (6, 7, 4):
+    for unit in (6, 7, 3):
         r.c(unit)
     values(3)
-    for unit in (2, 3, 5, 0, 1, 6, 4, 7):
+    for unit in (1, 2, 4, 5, 0, 6, 3, 7):
         r.d(unit)
     out[...] = jnp.swapaxes(r.fin[...], 0, 1)
     g.drain()

time: 55.6 us -> 50.8 us (0.914)
  Pallas kernels: 52.7 us -> 47.8 us
    pallas_call x1, Pallas kernels: 52.7 us -> 47.8 us  [on_device(): pl.pallas_call(kernel, out_shape=[pltpu.VMEM((1, 192, 2048), jnp.bfloat16...]
where the time goes in v4:
time: 50.8 us; the launch traced here: 49.9 us
  Pallas kernels  47.8 us (94%)
  local copies, waits for them, and re-layouts  1.54 us (3%)
  between operations  0.64 us (1%)
    pallas_call x1, Pallas kernels, on_device(): pl.pallas_call(kernel, out_shape=[pltpu.VMEM((1, 192, 2048), jnp.bfloat16...  47.8 us
    unnamed x2, local copies, waits for them, and re-layouts  1.54 us

profile of v4, /device:TPU:1, one launch (start us, length us, event | category | flops | bytes accessed | tf_op | source)
XLA Modules:
  0.0 49.9 jit_solution(3332656262803476359)
XLA Ops:
  0.6 47.8 %attention.1 = (bf16[1,192,2048]{2,1,0:T(8,128)(2,1)S(1)}, f32[16,16,128]{2,1,0:T(8,128)S(1)}) custom-call(s32[1,24]{1,0:T(1,128)} %order_hbm.1, s32[1,8]{1,0:T(1,128)} %lengths_hbm.1, bf16[1,24,512]{2,1,0:T(8,128)(2,1)} %lat_hbm.1, bf16[1,24,64]{2,1,0:T(8,128)(2,1)} %rope_hbm.1, bf16[1,192,16,512]{3,2,1,0:T(8,128)(2,1)} %q_hbm.1, ...), custom_call_target="tpu_custom_call" | custom-call | tf_op jit(solution)/shard_map/attention/pallas_call | solution.py:413
  48.4 0.9 %copy.12 = bf16[1,192,2048]{2,1,0:T(8,128)(2,1)} copy(bf16[1,192,2048]{2,1,0:T(8,128)(2,1)S(1)} %get-tuple-element.2) | data formatting | bytes 1572864
  49.3 0.7 %copy.13 = f32[16,16,128]{2,1,0:T(8,128)} copy(f32[16,16,128]{2,1,0:T(8,128)S(1)} %get-tuple-element.3) | data formatting | bytes 262144

commit v5 on v4

--- a/solution.py
+++ b/solution.py
@@ -288,8 +288,8 @@
 
 
 class Attend:
-    def __init__(self, order, lengths, q, qr, qt, keys, bias, u):
-        self.order, self.lengths, self.q, self.qr, self.qt, self.keys, self.bias, self.u = order, lengths, q, qr, qt, keys, bias, u
+    def __init__(self, order, lengths, q, qr, qt, keys, window, turned, bias, u):
+        self.order, self.lengths, self.q, self.qr, self.qt, self.keys, self.window, self.turned, self.bias, self.u = order, lengths, q, qr, qt, keys, window, turned, bias, u
         self.firsts = []
 
     def arrange(self):
@@ -316,10 +316,16 @@
             j = first + lax.broadcasted_iota(jnp.int32, (BLOCK, SPAN), 1)
             self.bias[b] = jnp.where((j >= low) & (j <= pos), 0.0, -1e30)
 
+    def windows(self):
+        for b in range(3):
+            k = self.keys[pl.ds(self.firsts[b], SPAN // 8)].reshape(SPAN, 640)
+            self.window[b] = k
+            self.turned[b] = k.T
+
     def block(self, head, n, b):
         q = self.qt[b, pl.ds(head, n)].reshape(n * BLOCK, 640)
-        k = self.keys[pl.ds(self.firsts[b], SPAN // 8)].reshape(SPAN, 640)
-        s = lax.dot_general(q, k, (((1,), (1,)), ((), ())), preferred_element_type=jnp.float32)
+        k = self.window[b]
+        s = jnp.dot(q, self.turned[b], preferred_element_type=jnp.float32)
         s = s.reshape(n, BLOCK, SPAN) + self.bias[b][None]
         top = jnp.max(s, axis=2, keepdims=True)
         p = jnp.exp2((s - top) * SCALE)
@@ -329,7 +335,7 @@
         self.u[pl.ds(head, n), b * BLOCK : (b + 1) * BLOCK, :] = (mixed.reshape(n, BLOCK, 512) / total).astype(jnp.bfloat16)
 
 
-def kernel(order_hbm, lengths_hbm, lat_hbm, rope_hbm, q_hbm, qr_hbm, do_hbm, w_hbm, attn, out, order, lengths, lat, rope, q, qr, do, w, loads, keys, send, recv, qt, bias, u, grad, *reduce_refs):
+def kernel(order_hbm, lengths_hbm, lat_hbm, rope_hbm, q_hbm, qr_hbm, do_hbm, w_hbm, attn, out, order, lengths, lat, rope, q, qr, do, w, loads, keys, send, recv, qt, window, turned, bias, u, grad, *reduce_refs):
     copies = [
         pltpu.make_async_copy(src, dst, loads.at[i])
         for i, (src, dst) in enumerate(
@@ -355,10 +361,11 @@
     g.begin()
     for c in copies[2:]:
         c.wait()
-    a = Attend(order, lengths, q, qr, qt, keys, bias, u)
+    a = Attend(order, lengths, q, qr, qt, keys, window, turned, bias, u)
     a.arrange()
     a.mask()
     g.run()
+    a.windows()
 
     def gradient(first, n):
         for h in range(n):
@@ -424,6 +431,8 @@
             pltpu.SemaphoreType.DMA((3,)),
             pltpu.SemaphoreType.DMA((Gather.COUNT,)),
             pltpu.VMEM((3, 16, BLOCK, 640), jnp.bfloat16),
+            pltpu.VMEM((3, SPAN, 640), jnp.bfloat16),
+            pltpu.VMEM((3, 640, SPAN), jnp.bfloat16),
             pltpu.VMEM((3, BLOCK, SPAN), jnp.float32),
             pltpu.VMEM((16, 192, 512), jnp.bfloat16),
             pltpu.VMEM((16, 512, 128), jnp.float32),

time: 50.8 us -> 50.8 us (level)
  no operation moved by 1% of the time
where the time goes in v5:
time: 50.8 us; the launch traced here: 50.2 us
  Pallas kernels  48 us (94%)
  local copies, waits for them, and re-layouts  1.54 us (3%)
  between operations  0.64 us (1%)
    pallas_call x1, Pallas kernels, on_device(): pl.pallas_call(kernel, out_shape=[pltpu.VMEM((1, 192, 2048), jnp.bfloat16...  48 us
    unnamed x2, local copies, waits for them, and re-layouts  1.54 us

profile of v5, /device:TPU:1, one launch (start us, length us, event | category | flops | bytes accessed | tf_op | source)
XLA Modules:
  0.0 50.2 jit_solution(8607298393717828869)
XLA Ops:
  0.6 48.0 %attention.1 = (bf16[1,192,2048]{2,1,0:T(8,128)(2,1)S(1)}, f32[16,16,128]{2,1,0:T(8,128)S(1)}) custom-call(s32[1,24]{1,0:T(1,128)} %order_hbm.1, s32[1,8]{1,0:T(1,128)} %lengths_hbm.1, bf16[1,24,512]{2,1,0:T(8,128)(2,1)} %lat_hbm.1, bf16[1,24,64]{2,1,0:T(8,128)(2,1)} %rope_hbm.1, bf16[1,192,16,512]{3,2,1,0:T(8,128)(2,1)} %q_hbm.1, ...), custom_call_target="tpu_custom_call" | custom-call | tf_op jit(solution)/shard_map/attention/pallas_call | solution.py:420
  48.6 0.9 %copy.12 = bf16[1,192,2048]{2,1,0:T(8,128)(2,1)} copy(bf16[1,192,2048]{2,1,0:T(8,128)(2,1)S(1)} %get-tuple-element.2) | data formatting | bytes 1572864
  49.5 0.7 %copy.13 = f32[16,16,128]{2,1,0:T(8,128)} copy(f32[16,16,128]{2,1,0:T(8,128)S(1)} %get-tuple-element.3) | data formatting | bytes 262144
